TPU v7x, 128 devices: a whole 4x4x4 slice. The times are simulated.
128 devices in a mesh: grp: 8 (over z, y_hi), blk: 16 (over y_lo, x, core).
Axes of the slice: x: 4, y: 4 (y_hi: 2, y_lo: 2; y = y_hi * 2 + y_lo), z: 4, core: 2. Of those that a mesh axis runs over, the one named last changes fastest.
Arguments:
- images: bfloat16 [131072, 1152], P(('grp', 'blk')), may hold values from -0.19921875 to 0.19921875
- texts: bfloat16 [131072, 1152], P(('grp', 'blk')), may hold values from -0.19921875 to 0.19921875
- log_logit_scale: float32 [1], replicated, may hold values from 1 to 2
- bias: float32 [1], replicated, may hold values from -3 to -1
Outputs:
- image_grad: float32 [131072, 1152], P(('grp', 'blk'))
- text_grad: float32 [131072, 1152], P(('grp', 'blk'))
All inputs are finite; a program needn't handle non-finite values.
Results may differ from a plain program's by a relative error of at most 0.0041.
Values may be sent and summed in bfloat16 or wider, within the bound.
No kernel may reach another device: no remote copies, remote signals or barrier semaphores. Data moves between devices by JAX's collectives and lax.ppermute only.
A program may use at most 128 MiB of HBM per device.

v0:
```python
import jax
import jax.numpy as jnp
from jax import lax
from jax.sharding import PartitionSpec as P

EPSILON = 1e-06


def passed_along(value, axis, steps):
    count = lax.axis_size(axis)
    pairs = [(source, (source + steps) % count) for source in range(count)]
    return lax.ppermute(value, axis, pairs)


def unit_rows(raw):
    values = raw.astype(jnp.float32)
    norms = jnp.sqrt(jnp.sum(values * values, axis=-1, keepdims=True) + EPSILON)
    return (values / norms, norms)


def block_pair_factor(
    image_lower_half, paired_block, scale_factor, block_distance, is_positive_pair
):
    pair_scores = (
        scale_factor
        * lax.dot_general(
            image_lower_half,
            paired_block,
            (((1,), (1,)), ((), ())),
            preferred_element_type=jnp.float32,
        )
        + block_distance
    )
    if is_positive_pair:
        target_sign = 2.0 * jnp.eye(image_lower_half.shape[0], dtype=jnp.float32) - 1.0
        pair_weight_factor = (
            scale_factor * -target_sign * jax.nn.sigmoid(-target_sign * pair_scores)
        )
    else:
        pair_weight_factor = scale_factor * jax.nn.sigmoid(pair_scores)
    return pair_weight_factor.astype(jnp.bfloat16)


def left_product(pair_weight_factor, paired_block):
    return jnp.dot(pair_weight_factor, paired_block, preferred_element_type=jnp.float32)


def right_product(pair_weight_factor, image_lower_half):
    return lax.dot_general(
        pair_weight_factor,
        image_lower_half,
        (((0,), (0,)), ((), ())),
        preferred_element_type=jnp.float32,
    )


def project_back(unit, norms, direction):
    return (direction - unit * jnp.sum(unit * direction, axis=-1, keepdims=True)) / norms


def body(images, texts, log_logit_scale, bias):
    scale_factor = jnp.exp(log_logit_scale[0])
    block_distance = bias[0]
    image_unit, image_norm = unit_rows(images)
    text_unit, text_norm = unit_rows(texts)
    image_lower_half = image_unit.astype(jnp.bfloat16)
    text_lower_half = text_unit.astype(jnp.bfloat16)
    passed = []
    current = text_lower_half
    for repeat in range(2):
        current = passed_along(current, "blk", 1)
        passed.append(current)
    text_adjacent, text_distant = (passed[0], passed[1])
    text_foreign = passed_along(text_lower_half, "grp", 1)
    local_factor = block_pair_factor(
        image_lower_half, text_lower_half, scale_factor, block_distance, True
    )
    image_dir = left_product(local_factor, text_lower_half)
    text_dir = right_product(local_factor, image_lower_half)
    adjacent_factor = block_pair_factor(
        image_lower_half, text_adjacent, scale_factor, block_distance, False
    )
    distant_factor = block_pair_factor(
        image_lower_half, text_distant, scale_factor, block_distance, False
    )
    foreign_factor = block_pair_factor(
        image_lower_half, text_foreign, scale_factor, block_distance, False
    )
    image_dir = image_dir + left_product(adjacent_factor, text_adjacent)
    image_dir = image_dir + left_product(distant_factor, text_distant)
    image_dir = image_dir + left_product(foreign_factor, text_foreign)
    near_terms = right_product(adjacent_factor, image_lower_half)
    far_terms = right_product(distant_factor, image_lower_half)
    other_terms = right_product(foreign_factor, image_lower_half)
    carried = far_terms
    for repeat in range(2):
        carried = passed_along(carried, "blk", -1)
        if repeat == 0:
            carried = carried + near_terms
    text_dir = text_dir + carried
    text_dir = text_dir + passed_along(other_terms.astype(jnp.bfloat16), "grp", -1).astype(
        other_terms.dtype
    )
    image_grad = project_back(image_unit, image_norm, image_dir)
    text_grad = project_back(text_unit, text_norm, text_dir)
    return (image_grad, text_grad)


def solution(mesh):
    return jax.shard_map(
        body,
        mesh=mesh,
        in_specs=(P(("grp", "blk"), None), P(("grp", "blk"), None), P(), P()),
        out_specs=(P(("grp", "blk"), None), P(("grp", "blk"), None)),
        check_vma=False,
    )
```

profile of v0, /device:TPU:7, one launch (start us, length us, event | category | flops | bytes accessed | tf_op | source)
XLA Modules:
  0.0 297.6 jit_solution(14548989653180370431)
XLA Ops:
  0.6 2.3 fusion.1
  3.0 2.4 fusion.3
  5.4 1.8 collective-permute-start
  7.3 25.8 %collective-permute-done = bf16[1024,1152]{1,0:T(8,128)(2,1)S(1)} collective-permute-done((bf16[1024,1152]{1,0:T(8,128)(2,1)S(1)}, bf16[1024,1152]{1,0:T(8,128)(2,1)S(1)}, u32[]{:S(2)}, u32[]{:S(2)}) %collective-permute-start) | collective-permute-done | bytes 2359328 | tf_op jit(solution)/shard_map/ppermute | solution.py:12
  33.1 4.6 %collective-permute-start.1 = (bf16[1024,1152]{1,0:T(8,128)(2,1)S(1)}, bf16[1024,1152]{1,0:T(8,128)(2,1)S(1)}, u32[]{:S(2)}, u32[]{:S(2)}) collective-permute-start(bf16[1024,1152]{1,0:T(8,128)(2,1)S(1)} %collective-permute-done), channel_id=1, source_target_pairs={{0,1},{1,2},{2,3},{3,4},{4,5},{5,6},{6,7},{7,8},{8,9},{9,10},{10,1... | collective-permute-start | bytes 7077896 | tf_op jit(solution)/shard_map/ppermute | solution.py:12
  40.3 23.1 %collective-permute-done.1 = bf16[1024,1152]{1,0:T(8,128)(2,1)S(1)} collective-permute-done((bf16[1024,1152]{1,0:T(8,128)(2,1)S(1)}, bf16[1024,1152]{1,0:T(8,128)(2,1)S(1)}, u32[]{:S(2)}, u32[]{:S(2)}) %collective-permute-start.1) | collective-permute-done | bytes 2359328 | tf_op jit(solution)/shard_map/ppermute | solution.py:12
  63.4 3.7 %multiply_convert_fusion.1 = bf16[1024,1024]{1,0:T(8,128)(2,1)S(1)} fusion(bf16[1024,1152]{1,0:T(8,128)(2,1)S(1)} %fusion.2, bf16[1024,1152]{1,0:T(8,128)(2,1)S(1)} %collective-permute-done.1, f32[]{:T(128)} %bitcast.28, f32[]{:T(128)} %bitcast), kind=kOutput, calls=%fused_computation.14 | convolution fusion | flops 2423259136 | bytes 6815752 | tf_op jit(solution)/shard_map/dot_general | solution.py:26
  67.2 3.0 %fusion.7 = f32[1024,1152]{1,0:T(8,128)S(1)} fusion(bf16[1024,1024]{1,0:T(8,128)(2,1)S(1)} %multiply_convert_fusion.1, bf16[1024,1152]{1,0:T(8,128)(2,1)S(1)} %fusion.2), kind=kOutput, calls=%fused_computation.26 | convolution fusion | flops 2415919104 | bytes 9175040 | tf_op jit(solution)/shard_map/dot_general | solution.py:49
  70.2 2.9 collective-permute-start.2
  73.1 4.5 %multiply_convert_fusion.3 = bf16[1024,1024]{1,0:T(8,128)(2,1)S(1)} fusion(bf16[1024,1152]{1,0:T(8,128)(2,1)S(1)} %fusion.2, bf16[1024,1152]{1,0:T(8,128)(2,1)S(1)} %fusion.3, f32[]{:T(128)} %bitcast.26, f32[]{:T(128)} %bitcast), kind=kOutput, calls=%fused_computation.16 | convolution fusion | flops 2429550592 | bytes 6815752 | tf_op jit(solution)/shard_map/dot_general | solution.py:26
  77.6 4.5 %fusion.4 = f32[1024,1152]{1,0:T(8,128)} fusion(bf16[1024,1024]{1,0:T(8,128)(2,1)S(1)} %multiply_convert_fusion.3, bf16[1024,1152]{1,0:T(8,128)(2,1)S(1)} %fusion.3), kind=kOutput, calls=%fused_computation.23 | convolution fusion | flops 2415919104 | bytes 9175040 | tf_op jit(solution)/shard_map/dot_general | solution.py:45
  82.1 3.7 %multiply_convert_fusion.2 = bf16[1024,1024]{1,0:T(8,128)(2,1)S(1)} fusion(bf16[1024,1152]{1,0:T(8,128)(2,1)S(1)} %fusion.2, bf16[1024,1152]{1,0:T(8,128)(2,1)S(1)} %collective-permute-done, f32[]{:T(128)} %bitcast.29, f32[]{:T(128)} %bitcast), kind=kOutput, calls=%fused_computation.15 | convolution fusion | flops 2423259136 | bytes 6815752 | tf_op jit(solution)/shard_map/dot_general | solution.py:26
  85.8 92.6 %collective-permute-done.2 = bf16[1024,1152]{1,0:T(8,128)(2,1)S(1)} collective-permute-done((bf16[1024,1152]{1,0:T(8,128)(2,1)S(1)}, bf16[1024,1152]{1,0:T(8,128)(2,1)S(1)}, u32[]{:S(2)}, u32[]{:S(2)}) %collective-permute-start.2) | collective-permute-done | bytes 2359328 | tf_op jit(solution)/shard_map/ppermute | solution.py:12
  178.4 3.7 %multiply_convert_fusion = bf16[1024,1024]{1,0:T(8,128)(2,1)S(1)} fusion(bf16[1024,1152]{1,0:T(8,128)(2,1)S(1)} %fusion.2, bf16[1024,1152]{1,0:T(8,128)(2,1)S(1)} %collective-permute-done.2, f32[]{:T(128)} %bitcast.27, f32[]{:T(128)} %bitcast), kind=kOutput, calls=%fused_computation.13 | convolution fusion | flops 2423259136 | bytes 6815752 | tf_op jit(solution)/shard_map/dot_general | solution.py:26
  182.2 3.1 %convolution_add_fusion = f32[1024,1152]{1,0:T(8,128)S(1)} fusion(f32[1024,1152]{1,0:T(8,128)S(1)} %collective-permute-done.3, bf16[1024,1024]{1,0:T(8,128)(2,1)S(1)} %multiply_convert_fusion.2, bf16[1024,1152]{1,0:T(8,128)(2,1)S(1)} %fusion.2), kind=kOutput, calls=%fused_computation.12 | convolution fusion | flops 2417098752 | bytes 13893632 | tf_op jit(solution)/shard_map/dot_general | solution.py:49
  185.8 3.2 %convolution_convert_fusion = bf16[1024,1152]{1,0:T(8,128)(2,1)S(1)} fusion(bf16[1024,1024]{1,0:T(8,128)(2,1)S(1)} %multiply_convert_fusion, bf16[1024,1152]{1,0:T(8,128)(2,1)S(1)} %fusion.2), kind=kOutput, calls=%fused_computation.18 | convolution fusion | flops 2417098752 | bytes 6815744 | tf_op jit(solution)/shard_map/dot_general | solution.py:49
  189.0 3.8 %collective-permute-start.5 = (bf16[1024,1152]{1,0:T(8,128)(2,1)S(1)}, bf16[1024,1152]{1,0:T(8,128)(2,1)S(1)}, u32[]{:S(2)}, u32[]{:S(2)}) collective-permute-start(bf16[1024,1152]{1,0:T(8,128)(2,1)S(1)} %convolution_convert_fusion), channel_id=1, source_target_pairs={{0,112},{16,0},{32,16},{48,32},{64,48},{80,64},{96,80},{112,96},{1... | collective-permute-start | bytes 7077896 | tf_op jit(solution)/shard_map/ppermute | solution.py:12
  192.8 4.5 %fusion.6 = f32[1024,1152]{1,0:T(8,128)} fusion(bf16[1024,1024]{1,0:T(8,128)(2,1)S(1)} %multiply_convert_fusion, bf16[1024,1152]{1,0:T(8,128)(2,1)S(1)} %collective-permute-done.2), kind=kOutput, calls=%fused_computation.25 | convolution fusion | flops 2415919104 | bytes 9175040 | tf_op jit(solution)/shard_map/dot_general | solution.py:45
  197.3 4.4 %fusion.5 = f32[1024,1152]{1,0:T(8,128)} fusion(bf16[1024,1024]{1,0:T(8,128)(2,1)S(1)} %multiply_convert_fusion.2, bf16[1024,1152]{1,0:T(8,128)(2,1)S(1)} %collective-permute-done), kind=kOutput, calls=%fused_computation.24 | convolution fusion | flops 2415919104 | bytes 9175040 | tf_op jit(solution)/shard_map/dot_general | solution.py:45
  201.7 9.2 %multiply_reduce_fusion.1 = (f32[1024]{0:T(1024)S(1)}, f32[1024,1152]{1,0:T(8,128)S(1)}) fusion(f32[1024]{0:T(1024)S(1)} %add_sqrt_fusion.1, bf16[1024,1152]{1,0:T(8,128)(2,1)S(1)} %copy-done, f32[1024,1152]{1,0:T(8,128)} %fusion.6, bf16[1024,1024]{1,0:T(8,128)(2,1)} %copy-done.2, bf16[1024,1152]{1,0:T(8,128)(2,1)S(1)} %collective-permute-done.1, ...), kind=kOutput, calls=%fused_computation.10 | convolution fusion | flops 2424175616 | bytes 25698304 | tf_op jit(solution)/shard_map/dot_general | solution.py:45
  211.0 3.0 subtract_divide_fusion.1
  213.9 76.5 %collective-permute-done.5 = bf16[1024,1152]{1,0:T(8,128)(2,1)S(1)} collective-permute-done((bf16[1024,1152]{1,0:T(8,128)(2,1)S(1)}, bf16[1024,1152]{1,0:T(8,128)(2,1)S(1)}, u32[]{:S(2)}, u32[]{:S(2)}) %collective-permute-start.5) | collective-permute-done | bytes 2359328 | tf_op jit(solution)/shard_map/ppermute | solution.py:12
  290.4 4.1 %multiply_reduce_fusion = (f32[1024]{0:T(1024)S(1)}, f32[1024,1152]{1,0:T(8,128)S(1)}) fusion(bf16[1024,1152]{1,0:T(8,128)(2,1)S(1)} %collective-permute-done.5, f32[1024,1152]{1,0:T(8,128)S(1)} %collective-permute-done.4, f32[1024]{0:T(1024)S(1)} %add_sqrt_fusion, bf16[1024,1152]{1,0:T(8,128)(2,1)S(1)} %copy-done.1, bf16[1024,1024]{1,0:T(8,128)(2,1)S(1)} %copy-done.4, ...), kind=kOutput, calls=%fused_computation.7 | convolution fusion | flops 2424175616 | bytes 18620416 | tf_op jit(solution)/shard_map/dot_general | solution.py:49
  294.5 3.1 %subtract_divide_fusion = f32[1024,1152]{1,0:T(8,128)} fusion(f32[1024]{0:T(1024)S(1)} %get-tuple-element.4, f32[1024]{0:T(1024)S(1)} %add_sqrt_fusion, bf16[1024,1152]{1,0:T(8,128)(2,1)S(1)} %collective-permute-done.5, f32[1024,1152]{1,0:T(8,128)S(1)} %get-tuple-element.5, f32[1024,1152]{1,0:T(8,128)S(1)} %collective-permute-done.4, ...), kind=kLoop, calls=%fused_computation.6 | loop fusion | flops 9437184 | bytes 18882560 | tf_op jit(solution)/shard_map/div | solution.py:58
  (18 shorter events, 1.9 us)
Async XLA Ops:
  0.6 38.4 %copy-start = (bf16[1024,1152]{1,0:T(8,128)(2,1)S(1)}, bf16[1024,1152]{1,0:T(8,128)(2,1)}, u32[]{:S(2)}) copy-start(bf16[1024,1152]{1,0:T(8,128)(2,1)} %param.4) | copy-start | bytes 7077892
  5.4 27.6 %collective-permute-start = (bf16[1024,1152]{1,0:T(8,128)(2,1)S(1)}, bf16[1024,1152]{1,0:T(8,128)(2,1)S(1)}, u32[]{:S(2)}, u32[]{:S(2)}) collective-permute-start(bf16[1024,1152]{1,0:T(8,128)(2,1)S(1)} %fusion.3), channel_id=1, source_target_pairs={{0,1},{1,2},{2,3},{3,4},{4,5},{5,6},{6,7},{7,8},{8,9},{9,10},{10,1... | collective-permute-start | bytes 7077896 | tf_op jit(solution)/shard_map/ppermute | solution.py:12
  33.1 30.4 %collective-permute-start.1 = (bf16[1024,1152]{1,0:T(8,128)(2,1)S(1)}, bf16[1024,1152]{1,0:T(8,128)(2,1)S(1)}, u32[]{:S(2)}, u32[]{:S(2)}) collective-permute-start(bf16[1024,1152]{1,0:T(8,128)(2,1)S(1)} %collective-permute-done), channel_id=1, source_target_pairs={{0,1},{1,2},{2,3},{3,4},{4,5},{5,6},{6,7},{7,8},{8,9},{9,10},{10,1... | collective-permute-start | bytes 7077896 | tf_op jit(solution)/shard_map/ppermute | solution.py:12
  67.2 10.4 %copy-start.2 = (bf16[1024,1024]{1,0:T(8,128)(2,1)}, bf16[1024,1024]{1,0:T(8,128)(2,1)S(1)}, u32[]{:S(2)}) copy-start(bf16[1024,1024]{1,0:T(8,128)(2,1)S(1)} %multiply_convert_fusion.1) | copy-start | bytes 6291460
  70.2 112.0 %collective-permute-start.3 = (f32[1024,1152]{1,0:T(8,128)S(1)}, f32[1024,1152]{1,0:T(8,128)S(1)}, u32[]{:S(2)}, u32[]{:S(2)}) collective-permute-start(f32[1024,1152]{1,0:T(8,128)S(1)} %fusion.7), channel_id=1, source_target_pairs={{0,15},{1,0},{2,1},{3,2},{4,3},{5,4},{6,5},{7,6},{8,7},{9,8},{10,9... | collective-permute-start | bytes 14155784 | tf_op jit(solution)/shard_map/ppermute | solution.py:12
  70.2 108.2 %collective-permute-start.2 = (bf16[1024,1152]{1,0:T(8,128)(2,1)S(1)}, bf16[1024,1152]{1,0:T(8,128)(2,1)S(1)}, u32[]{:S(2)}, u32[]{:S(2)}) collective-permute-start(bf16[1024,1152]{1,0:T(8,128)(2,1)S(1)} %fusion.3), channel_id=1, source_target_pairs={{0,16},{16,32},{32,48},{48,64},{64,80},{80,96},{96,112},{112,0},{1... | collective-permute-start | bytes 7077896 | tf_op jit(solution)/shard_map/ppermute | solution.py:12
  77.6 4.5 %copy-start.3 = (bf16[1024,1024]{1,0:T(8,128)(2,1)}, bf16[1024,1024]{1,0:T(8,128)(2,1)S(1)}, u32[]{:S(2)}) copy-start(bf16[1024,1024]{1,0:T(8,128)(2,1)S(1)} %multiply_convert_fusion.3) | copy-start | bytes 6291460
  185.3 105.1 %collective-permute-start.4 = (f32[1024,1152]{1,0:T(8,128)S(1)}, f32[1024,1152]{1,0:T(8,128)S(1)}, u32[]{:S(2)}, u32[]{:S(2)}) collective-permute-start(f32[1024,1152]{1,0:T(8,128)S(1)} %convolution_add_fusion), channel_id=1, source_target_pairs={{0,15},{1,0},{2,1},{3,2},{4,3},{5,4},{6,5},{7,6},{8,7},{9,8},{10,9... | collective-permute-start | bytes 14155784 | tf_op jit(solution)/shard_map/ppermute | solution.py:12
  189.0 101.4 %collective-permute-start.5 = (bf16[1024,1152]{1,0:T(8,128)(2,1)S(1)}, bf16[1024,1152]{1,0:T(8,128)(2,1)S(1)}, u32[]{:S(2)}, u32[]{:S(2)}) collective-permute-start(bf16[1024,1152]{1,0:T(8,128)(2,1)S(1)} %convolution_convert_fusion), channel_id=1, source_target_pairs={{0,112},{16,0},{32,16},{48,32},{64,48},{80,64},{96,80},{112,96},{1... | collective-permute-start | bytes 7077896 | tf_op jit(solution)/shard_map/ppermute | solution.py:12
  210.9 79.5 %copy-start.1 = (bf16[1024,1152]{1,0:T(8,128)(2,1)S(1)}, bf16[1024,1152]{1,0:T(8,128)(2,1)}, u32[]{:S(2)}) copy-start(bf16[1024,1152]{1,0:T(8,128)(2,1)} %param.5) | copy-start | bytes 7077892
  210.9 79.5 %copy-start.4 = (bf16[1024,1024]{1,0:T(8,128)(2,1)S(1)}, bf16[1024,1024]{1,0:T(8,128)(2,1)}, u32[]{:S(2)}) copy-start(bf16[1024,1024]{1,0:T(8,128)(2,1)} %copy-done.3) | copy-start | bytes 6291460
where the time goes:
time: 298 us
  waiting for transfers between devices  218 us (73%)
  matrix products  51.7 us (17%)
  starting transfers between devices  13.6 us (5%)
  other arithmetic  12.1 us (4%)
    ppermute x6, waiting for transfers between devices, passed_along(): return lax.ppermute(value, axis, pairs)  218 us
    dot_general x4, matrix products, left_product(): jnp.dot(pair_weight_factor, paired_block, preferred_element_type=jnp.floa...  22.6 us
    dot_general x4, matrix products, block_pair_factor(): lax.dot_general(image_lower_half, paired_block, (((1,), (1,)), ((), ())),...  15.6 us
    ppermute x6, starting transfers between devices, passed_along(): return lax.ppermute(value, axis, pairs)  13.6 us
    dot_general x4, matrix products, right_product(): lax.dot_general(pair_weight_factor, image_lower_half, (((0,), (0,)), ((),...  13.5 us
    div x2, other arithmetic, project_back(): (direction - unit * jnp.sum(unit * direction, axis=-1, keepdims=True)) /...  6.02 us
  transfers between devices with their start and end apart: 6, of which 4 were waited for; matrix products, arithmetic and copies ran while one was open for 14% of the time, Pallas kernels for 0%

commit v1 on v0

v1 whole, which is shorter than its diff:
```python
import functools

import jax
import jax.numpy as jnp
from jax import lax
from jax.experimental import pallas as pl
from jax.experimental.pallas import tpu as pltpu
from jax.sharding import PartitionSpec as P

EPSILON = 1e-06
D = 1152
ROWS = 1024
HALF = 512
TILE = 256
AXES = ("grp", "blk")
WIDE = 384
VMEM_LIMIT = 50 * 1024 * 1024
COST = pl.CostEstimate(flops=0, bytes_accessed=0, transcendentals=0)


def device(z, y, x, c):
    return (((z % 4) * 4 + y % 4) * 4 + x % 4) * 2 + c


def route(target):
    pairs = []
    for z in range(4):
        for y in range(4):
            for x in range(4):
                for c in range(2):
                    pairs.append((device(z, y, x, c), device(*target(z, y, x, c))))
    return pairs


def inner_first(is_text, x):
    return (x >= 2) == is_text


def first_hop(is_text):
    def target(z, y, x, c):
        return (z, y ^ 1 if inner_first(is_text(c), x) else 3 - y, x, c)

    return target


def second_hop(is_text):
    def target(z, y, x, c):
        inner = inner_first(is_text(c), x)
        origin = y ^ 1 if inner else 3 - y
        to = 3 - y if inner else y ^ 1
        if is_text(c):
            z += 1 if origin >= 2 else 0
        else:
            z -= 1 if origin < 2 else 0
        return (z, to, x, c)

    return target


def along(is_text):
    return lambda z, y, x, c: (z, y, x + 1 if is_text(c) else x - 1, c)


def other_core(z, y, x, c):
    return (z, y, x, 1 - c)


def a_is_text(c):
    return c == 1


def b_is_text(c):
    return c == 0


def send(name, value, target):
    with jax.named_scope(name):
        return lax.ppermute(value, AXES, route(target))


def after(values, *others):
    held = lax.optimization_barrier((tuple(values), tuple(others)))
    return held[0]


def normalized(raw):
    values = raw.astype(jnp.float32)
    inverse = 1.0 / jnp.sqrt(jnp.sum(values * values, axis=-1, keepdims=True) + EPSILON)
    return values * inverse, inverse


def all_rows_kernel(core, images, texts, a, b, a_0, b_0, a_1, b_1, image_inverse, text_inverse):
    image_unit, inverse = normalized(images[...])
    image_unit = image_unit.astype(jnp.bfloat16)
    image_inverse[...] = inverse
    text_unit, inverse = normalized(texts[...])
    text_unit = text_unit.astype(jnp.bfloat16)
    text_inverse[...] = inverse
    a_value = jnp.where(core[0] == 0, image_unit, text_unit)
    b_value = jnp.where(core[0] == 0, text_unit, image_unit)
    a[...] = a_value
    b[...] = b_value
    a_1[...] = a_value
    b_1[...] = b_value

    @pl.when(pl.program_id(0) == 0)
    def _():
        a_0[...] = a_value
        b_0[...] = b_value


def all_rows(core, images, texts):
    spec = pl.BlockSpec((HALF, D), lambda i: (i, 0))
    part_spec = pl.BlockSpec((HALF, D), lambda i: (0, 0))
    column = pl.BlockSpec((HALF, 1), lambda i: (i, 0))
    whole = jax.ShapeDtypeStruct((ROWS, D), jnp.bfloat16)
    part = jax.ShapeDtypeStruct((HALF, D), jnp.bfloat16)
    scale = jax.ShapeDtypeStruct((ROWS, 1), jnp.float32)
    return pl.pallas_call(
        all_rows_kernel,
        grid=(2,),
        in_specs=[pl.BlockSpec(memory_space=pltpu.SMEM), spec, spec],
        out_specs=[spec, spec] + [part_spec] * 4 + [column, column],
        out_shape=[whole, whole] + [part] * 4 + [scale, scale],
        compiler_params=pltpu.CompilerParams(vmem_limit_bytes=VMEM_LIMIT),
        cost_estimate=COST,
    )(core, images, texts)


def coefficients(dots, scalars, diagonal_at=None):
    bent = jnp.tanh(dots * scalars[0] + scalars[1])
    if diagonal_at is None:
        return ((bent + 1.0) * scalars[0]).astype(jnp.bfloat16)
    down = lax.broadcasted_iota(jnp.int32, dots.shape, 0)
    across = lax.broadcasted_iota(jnp.int32, dots.shape, 1) + diagonal_at
    return ((bent + jnp.where(across == down, -1.0, 1.0)) * scalars[0]).astype(jnp.bfloat16)


def row_dots(own, paired):
    return lax.dot_general(own, paired, (((1,), (1,)), ((), ())), preferred_element_type=jnp.float32)


def pairs_kernel(count, has_own, has_before, scalars, own, *refs):
    partners = refs[:count]
    total, factors = refs[count + has_before : count + has_before + 2]
    step = pl.program_id(0)

    def columns(part):
        return slice(part * WIDE, (part + 1) * WIDE)

    if has_before:
        before = refs[count]
        held, arrived = refs[-2:]
        loads = [
            pltpu.make_async_copy(before.at[:, columns(part)], held.at[:, columns(part)], arrived.at[part])
            for part in range(D // WIDE)
        ]

        @pl.when(step == 0)
        def _():
            for load in loads:
                load.start()

    base = 0
    for at, partner in enumerate(partners):
        def make(at=at, partner=partner, base=base):
            for start in range(0, partner.shape[0], TILE):
                dots = row_dots(own[...], partner[start : start + TILE, :])
                diagonal_at = start if has_own and at == 0 else None
                factors[:, base + start : base + start + TILE] = coefficients(dots, scalars, diagonal_at)

        pl.when(step == at)(make)
        base += partner.shape[0]

    for part in range(D // WIDE):
        def add(part=part):
            result = None
            if has_before:
                loads[part].wait()
                result = held[:, columns(part)]
            base = 0
            for partner in partners:
                rows = partner.shape[0]
                term = jnp.dot(factors[:, base : base + rows], partner[:, columns(part)], preferred_element_type=jnp.float32)
                result = term if result is None else result + term
                base += rows
            total[...] = result

        pl.when(step == count + part)(add)


def pairs(scalars, own, partners, before=None, has_own=False):
    count = len(partners)
    rows = sum(partner.shape[0] for partner in partners)
    once = pl.Buffered(1)
    has_before = before is not None
    return pl.pallas_call(
        functools.partial(pairs_kernel, count, has_own, int(has_before)),
        grid=(count + D // WIDE,),
        in_specs=[
            pl.BlockSpec(memory_space=pltpu.SMEM),
            pl.BlockSpec((ROWS, D), lambda i: (0, 0), pipeline_mode=once),
            *[pl.BlockSpec(partner.shape, lambda i: (0, 0), pipeline_mode=once) for partner in partners],
            *([pl.BlockSpec(memory_space=pl.ANY)] if has_before else []),
        ],
        out_specs=pl.BlockSpec((ROWS, WIDE), lambda i: (0, jnp.maximum(i - count, 0))),
        out_shape=jax.ShapeDtypeStruct((ROWS, D), jnp.float32),
        scratch_shapes=[
            pltpu.VMEM((ROWS, rows), jnp.bfloat16),
            *([pltpu.VMEM((ROWS, D), jnp.float32), pltpu.SemaphoreType.DMA((D // WIDE,))] if has_before else []),
        ],
        compiler_params=pltpu.CompilerParams(vmem_limit_bytes=VMEM_LIMIT),
        cost_estimate=COST,
    )(scalars, own, *partners, *([before] if has_before else []))


def last_kernel(core, scalars, a_pair, b_pair, images, texts, image_inverse, text_inverse, a_before, b_before, image_grad, text_grad):
    is_zero = core[0] == 0
    image_unit = images[...].astype(jnp.float32) * image_inverse[...]
    text_unit = texts[...].astype(jnp.float32) * text_inverse[...]
    grads = []
    for unit, scale, paired, before in (
        (jnp.where(is_zero, image_unit, text_unit), jnp.where(is_zero, image_inverse[...], text_inverse[...]), a_pair, a_before),
        (jnp.where(is_zero, text_unit, image_unit), jnp.where(is_zero, text_inverse[...], image_inverse[...]), b_pair, b_before),
    ):
        own = unit.astype(jnp.bfloat16)
        total = before[...]
        for start in range(0, paired.shape[0], TILE):
            rows = paired[start : start + TILE, :]
            factor = coefficients(row_dots(own, rows), scalars)
            total = total + jnp.dot(factor, rows, preferred_element_type=jnp.float32)
        inside = jnp.sum(unit * total, axis=-1, keepdims=True)
        grads.append((total - unit * inside) * scale)
    image_grad[...] = jnp.where(is_zero, grads[0], grads[1])
    text_grad[...] = jnp.where(is_zero, grads[1], grads[0])


def last_pairs(core, scalars, a_pair, b_pair, images, texts, image_inverse, text_inverse, a_before, b_before):
    rows = a_pair.shape[0]
    spec = pl.BlockSpec((TILE, D), lambda i: (i, 0))
    column = pl.BlockSpec((TILE, 1), lambda i: (i, 0))
    pair = pl.BlockSpec((rows, D), lambda i: (0, 0))
    grad = jax.ShapeDtypeStruct((ROWS, D), jnp.float32)
    scalar = pl.BlockSpec(memory_space=pltpu.SMEM)
    return pl.pallas_call(
        last_kernel,
        grid=(ROWS // TILE,),
        in_specs=[scalar, scalar, pair, pair, spec, spec, column, column, spec, spec],
        out_specs=[spec, spec],
        out_shape=[grad, grad],
        compiler_params=pltpu.CompilerParams(vmem_limit_bytes=VMEM_LIMIT),
        cost_estimate=COST,
    )(core, scalars, a_pair, b_pair, images, texts, image_inverse, text_inverse, a_before, b_before)


def body(images, texts, log_logit_scale, bias):
    scalars = 0.5 * jnp.concatenate([jnp.exp(log_logit_scale), bias])
    index = lax.axis_index(AXES).astype(jnp.int32)
    core = lax.rem(index, 2)
    x = lax.rem(lax.div(index, 2), 4)
    which = jnp.reshape(core, (1,))
    text_end, image_end = x == 3, x == 0
    a_end = jnp.where(core == 0, image_end, text_end)
    b_end = jnp.where(core == 0, text_end, image_end)

    a, b, a_0, b_0, a_1, b_1, image_inverse, text_inverse = all_rows(which, images, texts)
    a_01 = send("a_01", a_0, first_hop(a_is_text))
    b_01 = send("b_01", b_0, first_hop(b_is_text))
    near = send("near", b, other_core)
    a_sum = pairs(scalars, a, [b], has_own=True)
    b_sum = pairs(scalars, b, [a, near], has_own=True)

    a_1, b_1, a_sum, b_sum = after((a_1, b_1, a_sum, b_sum))
    a_11 = send("a_11", a_1, first_hop(a_is_text))
    b_11 = send("b_11", b_1, first_hop(b_is_text))
    a_01, b_01, b_sum = after((a_01, b_01, b_sum))
    a_x0 = send("a_x0", jnp.where(a_end, a_01, a_0), along(a_is_text))
    b_x0 = send("b_x0", jnp.where(b_end, b_01, b_0), along(b_is_text))

    a_01, b_01 = after((a_01, b_01), a_11, b_11)
    a_02 = send("a_02", a_01, second_hop(a_is_text))
    b_02 = send("b_02", b_01, second_hop(b_is_text))
    a_x1 = send("a_x1", jnp.where(a_end, a_11, a_1), along(a_is_text))
    b_x1 = send("b_x1", jnp.where(b_end, b_11, b_1), along(b_is_text))
    far_0 = send("far_0", a_x0, other_core)
    b_sum = pairs(scalars, b, [a_x0], b_sum)
    a_sum = pairs(scalars, a, [b_x0, far_0], a_sum)

    a_11, b_11, a_sum, b_sum = after((a_11, b_11, a_sum, b_sum), a_02, b_02)
    a_12 = send("a_12", a_11, second_hop(a_is_text))
    b_12 = send("b_12", b_11, second_hop(b_is_text))
    far_1 = send("far_1", a_x1, other_core)
    b_sum = pairs(scalars, b, [a_02, a_x1], b_sum)
    a_sum = pairs(scalars, a, [b_02, b_x1, far_1], a_sum)

    return tuple(
        last_pairs(which, scalars, b_12, a_12, images, texts, image_inverse, text_inverse, a_sum, b_sum)
    )


def solution(mesh):
    return jax.shard_map(
        body,
        mesh=mesh,
        in_specs=(P(AXES, None), P(AXES, None), P(), P()),
        out_specs=(P(AXES, None), P(AXES, None)),
        check_vma=False,
    )
```

time: 298 us -> 156 us (0.52)
  waiting for transfers between devices: 218 us -> 31.2 us
  Pallas kernels: 0 us -> 90.7 us
  matrix products: 51.7 us -> 0 us
  other arithmetic: 12.1 us -> 6.75 us
  starting transfers between devices: 13.6 us -> 18.6 us
  local copies, waits for them, and re-layouts: 0.02 us -> 3.26 us
    ppermute x6 -> x15, waiting for transfers between devices: 218 us -> 31.2 us  [send(): return lax.ppermute(value, AXES, route(target))]
    pallas_call x0 -> x8, Pallas kernels: none -> 90.7 us  [the longest x6 67.7 us: pairs(): pl.pallas_call(functools.partial(pairs_kernel, count, has_own, int(has_be...]
    dot_general x12 -> x0, matrix products: 51.7 us -> none  [the longest x4 22.6 us: left_product(): jnp.dot(pair_weight_factor, paired_block, preferred_element_type=jnp.floa...]
    select_n x0 -> x4, other arithmetic: none -> 6.67 us  [the longest x1 2.44 us: body(): a_x0 = send('a_x0', jnp.where(a_end, a_01, a_0), along(a_is_text))]
    div x2 -> x0, other arithmetic: 6.02 us -> none  [project_back(): (direction - unit * jnp.sum(unit * direction, axis=-1, keepdims=True)) /...]
    ppermute x6 -> x15, starting transfers between devices: 13.6 us -> 18.6 us  [send(): return lax.ppermute(value, AXES, route(target))]
    unnamed x10 -> x14, local copies, waits for them, and re-layouts: 0.02 us -> 3.26 us
    convert_element_type x2 -> x0, other arithmetic: 3.21 us -> none  [the longest x1 2.42 us: body(): text_lower_half = text_unit.astype(jnp.bfloat16)]
  transfers between devices with their start and end apart: 6 -> 15, of which waited for: 4 -> 5; matrix products, arithmetic and copies ran while one was open for 14% -> 4% of each run, Pallas kernels for 0% -> 44%
where the time goes in v1:
time: 156 us; the launch traced here: 153 us
  Pallas kernels  90.7 us (58%)
  waiting for transfers between devices  31.2 us (20%)
  starting transfers between devices  18.6 us (12%)
  other arithmetic  6.75 us (4%)
  local copies, waits for them, and re-layouts  3.26 us (2%)
  between operations  2.54 us (2%)
    pallas_call x6, Pallas kernels, pairs(): pl.pallas_call(functools.partial(pairs_kernel, count, has_own, int(has_be...  67.7 us
    ppermute x15, waiting for transfers between devices, send(): return lax.ppermute(value, AXES, route(target))  31.2 us
    ppermute x15, starting transfers between devices, send(): return lax.ppermute(value, AXES, route(target))  18.6 us
    pallas_call x1, Pallas kernels, last_pairs(): pl.pallas_call(last_kernel, grid=(ROWS // TILE,), in_specs=[scalar, scala...  15.9 us
    pallas_call x1, Pallas kernels, all_rows(): pl.pallas_call(all_rows_kernel, grid=(2,), in_specs=[pl.BlockSpec(memory_...  7.15 us
    unnamed x14, local copies, waits for them, and re-layouts  3.26 us
  transfers between devices with their start and end apart: 15, of which 5 were waited for; matrix products, arithmetic and copies ran while one was open for 4% of the time, Pallas kernels for 44%

profile of v1, /device:TPU:7, one launch (start us, length us, event | category | flops | bytes accessed | tf_op | source)
XLA Modules:
  0.0 153.0 jit_solution(6731365814294114784)
XLA Ops:
  0.6 7.2 %shard_map.59 = (bf16[1024,1152]{1,0:T(8,128)(2,1)}, bf16[1024,1152]{1,0:T(8,128)(2,1)}, bf16[512,1152]{1,0:T(8,128)(2,1)}, bf16[512,1152]{1,0:T(8,128)(2,1)S(1)...) custom-call(s32[1]{0:T(128)} %bitcast.core, ...), custom_call_target="tpu_custom_call" | custom-call | tf_op jit(solution)/shard_map/pallas_call | solution.py:119
  10.1 1.3 collective-permute-start.3
  11.4 2.1 %collective-permute-start.4 = (bf16[512,1152]{1,0:T(8,128)(2,1)S(1)}, bf16[512,1152]{1,0:T(8,128)(2,1)}, u32[]{:S(2)}, u32[]{:S(2)}) collective-permute-start(bf16[512,1152]{1,0:T(8,128)(2,1)S(1)} %get-tuple-element.30), channel_id=1, source_target_pairs={{0,24},{1,9},{2,26},{3,11},{4,12},{5,29},{6,14},{7,31},{8,16},{9,1... | collective-permute-start | bytes 3538952 | tf_op jit(solution)/shard_map/b_01/ppermute | solution.py:78
  14.8 1.7 %copy-done.1 = bf16[1024,1152]{1,0:T(8,128)(2,1)S(1)} copy-done((bf16[1024,1152]{1,0:T(8,128)(2,1)S(1)}, bf16[1024,1152]{1,0:T(8,128)(2,1)}, u32[]{:S(2)}) %copy-start.1) | copy-done | bytes 2359320
  16.5 9.9 %shard_map.60.refs_2_ = f32[1024,1152]{1,0:T(8,128)} custom-call(f32[2]{0:T(128)S(1)} %maximum_multiply_fusion.scalars, bf16[1024,1152]{1,0:T(8,128)(2,1)S(1)} %copy-done.1, bf16[1024,1152]{1,0:T(8,128)(2,1)} %get-tuple-element.26.refs_0_.own), custom_call_target="tpu_custom_call" | custom-call | tf_op jit(solution)/shard_map/pallas_call | solution.py:197
  26.4 16.9 %shard_map.61.refs_1_ = f32[1024,1152]{1,0:T(8,128)} custom-call(f32[2]{0:T(128)S(1)} %maximum_multiply_fusion.scalars, bf16[1024,1152]{1,0:T(8,128)(2,1)S(1)} %copy-done, bf16[1024,1152]{1,0:T(8,128)(2,1)} %get-tuple-element.25.own.refs_0_, bf16[1024,1152]{1,0:T(8,128)(2,1)} %collective-permute-done.refs_1_), custom_call_target="tpu_custom_call" | custom-call | tf_op jit(solution)/shard_map/pallas_call | solution.py:197
  44.6 2.4 %broadcast_select_fusion.1 = bf16[512,1152]{1,0:T(8,128)(2,1)} fusion(bf16[512,1152]{1,0:T(8,128)(2,1)} %collective-permute-done.3, bf16[512,1152]{1,0:T(8,128)(2,1)} %get-tuple-element.29, pred[]{:T(512)S(6)} %select_n.32), kind=kLoop, calls=%fused_computation.1 | loop fusion | flops 589824 | bytes 3538945 | tf_op jit(solution)/shard_map/jit(_where)/select_n | solution.py:277
  47.3 1.4 broadcast_select_fusion.3
  48.8 1.3 collective-permute-start.5
  50.0 20.0 %collective-permute-done.1 = bf16[512,1152]{1,0:T(8,128)(2,1)} collective-permute-done((bf16[512,1152]{1,0:T(8,128)(2,1)}, bf16[512,1152]{1,0:T(8,128)(2,1)}, u32[]{:S(2)}, u32[]{:S(2)}) %collective-permute-start.1) | collective-permute-done | bytes 1179680 | tf_op jit(solution)/shard_map/a_11/ppermute | solution.py:78
  70.0 3.3 %collective-permute-done.2 = bf16[512,1152]{1,0:T(8,128)(2,1)} collective-permute-done((bf16[512,1152]{1,0:T(8,128)(2,1)}, bf16[512,1152]{1,0:T(8,128)(2,1)}, u32[]{:S(2)}, u32[]{:S(2)}) %collective-permute-start.2) | collective-permute-done | bytes 1179680 | tf_op jit(solution)/shard_map/b_11/ppermute | solution.py:78
  74.1 4.3 %collective-permute-start.7 = (bf16[512,1152]{1,0:T(8,128)(2,1)S(1)}, bf16[512,1152]{1,0:T(8,128)(2,1)S(1)}, u32[]{:S(2)}, u32[]{:S(2)}) collective-permute-start(bf16[512,1152]{1,0:T(8,128)(2,1)S(1)} %collective-permute-done.6.refs_0_), channel_id=1, source_target_pairs={{0,1},{1,0},{2,3},{3,2},{4,5},{5,4},{6,7},{7,6},{8,9},{9,8},{10,11... | collective-permute-start | bytes 3538952 | tf_op jit(solution)/shard_map/far_0/ppermute | solution.py:78
  78.4 1.4 broadcast_select_fusion
  79.9 6.9 %shard_map.63.refs_2_ = f32[1024,1152]{1,0:T(8,128)} custom-call(f32[2]{0:T(128)S(1)} %maximum_multiply_fusion.scalars, bf16[1024,1152]{1,0:T(8,128)(2,1)S(1)} %copy-done, bf16[512,1152]{1,0:T(8,128)(2,1)S(1)} %collective-permute-done.6.refs_0_, f32[1024,1152]{1,0:T(8,128)} %shard_map.61.refs_1_), custom_call_target="tpu_custom_call" | custom-call | tf_op jit(solution)/shard_map/pallas_call | solution.py:197
  86.9 1.4 broadcast_select_fusion.2
  88.3 1.5 collective-permute-start.12
  89.8 10.1 %shard_map.62.refs_3_ = f32[1024,1152]{1,0:T(8,128)} custom-call(f32[2]{0:T(128)S(1)} %maximum_multiply_fusion.scalars, bf16[1024,1152]{1,0:T(8,128)(2,1)} %get-tuple-element.25.own.refs_0_, bf16[512,1152]{1,0:T(8,128)(2,1)S(1)} %collective-permute-done.5.refs_0_, bf16[512,1152]{1,0:T(8,128)(2,1)S(1)} %collective-permute-done.7.refs_1_, ...), custom_call_target="tpu_custom_call" | custom-call | tf_op jit(solution)/shard_map/pallas_call | solution.py:197
  99.9 3.6 %collective-permute-done.8.refs_0_ = bf16[512,1152]{1,0:T(8,128)(2,1)S(1)} collective-permute-done((bf16[512,1152]{1,0:T(8,128)(2,1)}, bf16[512,1152]{1,0:T(8,128)(2,1)S(1)}, u32[]{:S(2)}, u32[]{:S(2)}) %collective-permute-start.8) | collective-permute-done | bytes 1179680 | tf_op jit(solution)/shard_map/a_02/ppermute | solution.py:78
  103.4 1.7 %collective-permute-start.14 = (bf16[512,1152]{1,0:T(8,128)(2,1)S(1)}, bf16[512,1152]{1,0:T(8,128)(2,1)S(1)}, u32[]{:S(2)}, u32[]{:S(2)}) collective-permute-start(bf16[512,1152]{1,0:T(8,128)(2,1)S(1)} %collective-permute-done.13.refs_1_), channel_id=1, source_target_pairs={{0,1},{1,0},{2,3},{3,2},{4,5},{5,4},{6,7},{7,6},{8,9},{9,8},{10,11... | collective-permute-start | bytes 3538952 | tf_op jit(solution)/shard_map/far_1/ppermute | solution.py:78
  105.1 3.3 %collective-permute-start.11 = (bf16[512,1152]{1,0:T(8,128)(2,1)}, bf16[512,1152]{1,0:T(8,128)(2,1)S(1)}, u32[]{:S(2)}, u32[]{:S(2)}) collective-permute-start(bf16[512,1152]{1,0:T(8,128)(2,1)} %collective-permute-done.1), channel_id=1, source_target_pairs={{0,120},{1,41},{2,122},{3,43},{4,12},{5,29},{6,14},{7,31},{8,112},... | collective-permute-start | bytes 3538952 | tf_op jit(solution)/shard_map/a_12/ppermute | solution.py:78
  108.4 10.2 %shard_map.65.b_before = f32[1024,1152]{1,0:T(8,128)} custom-call(f32[2]{0:T(128)S(1)} %maximum_multiply_fusion.scalars, bf16[1024,1152]{1,0:T(8,128)(2,1)} %get-tuple-element.26.refs_0_.own, bf16[512,1152]{1,0:T(8,128)(2,1)S(1)} %collective-permute-done.8.refs_0_, bf16[512,1152]{1,0:T(8,128)(2,1)S(1)} %collective-permute-done.13.refs_1_, ...), custom_call_target="tpu_custom_call" | custom-call | tf_op jit(solution)/shard_map/pallas_call | solution.py:197
  118.7 13.6 %shard_map.64.a_before = f32[1024,1152]{1,0:T(8,128)} custom-call(f32[2]{0:T(128)S(1)} %maximum_multiply_fusion.scalars, bf16[1024,1152]{1,0:T(8,128)(2,1)} %get-tuple-element.25.own.refs_0_, bf16[512,1152]{1,0:T(8,128)(2,1)S(1)} %collective-permute-done.9.refs_0_, bf16[512,1152]{1,0:T(8,128)(2,1)S(1)} %collective-permute-done.12.refs_1_, ...), custom_call_target="tpu_custom_call" | custom-call | tf_op jit(solution)/shard_map/pallas_call | solution.py:197
  132.6 4.1 %collective-permute-done.11.b_pair = bf16[512,1152]{1,0:T(8,128)(2,1)S(1)} collective-permute-done((bf16[512,1152]{1,0:T(8,128)(2,1)}, bf16[512,1152]{1,0:T(8,128)(2,1)S(1)}, u32[]{:S(2)}, u32[]{:S(2)}) %collective-permute-start.11) | collective-permute-done | bytes 1179680 | tf_op jit(solution)/shard_map/a_12/ppermute | solution.py:78
  136.7 15.9 %shard_map.66 = (f32[1024,1152]{1,0:T(8,128)}, f32[1024,1152]{1,0:T(8,128)}) custom-call(s32[1]{0:T(128)} %bitcast.core, f32[2]{0:T(128)S(1)} %maximum_multiply_fusion.scalars, bf16[512,1152]{1,0:T(8,128)(2,1)S(1)} %collective-permute-done.10.a_pair, bf16[512,1152]{1,0:T(8,128)(2,1)S(1)} %collective-permute-done.11.b_pair, bf16[1024,1152]{1,0:T(8,128)(2,1)} %images.3, ...), custom_call_target="tpu_custom_call" | custom-call | tf_op jit(solution)/shard_map/pallas_call | solution.py:245
  (33 shorter events, 5.2 us)
Async XLA Ops:
  7.8 0.8 copy-start.3
  8.6 0.8 copy-start.5
  9.4 17.0 %copy-start.2 = (bf16[512,1152]{1,0:T(8,128)(2,1)}, bf16[512,1152]{1,0:T(8,128)(2,1)S(1)}, u32[]{:S(2)}) copy-start(bf16[512,1152]{1,0:T(8,128)(2,1)S(1)} %get-tuple-element.30) | copy-start | bytes 3538948
  9.4 17.0 %collective-permute-start = (bf16[1024,1152]{1,0:T(8,128)(2,1)}, bf16[1024,1152]{1,0:T(8,128)(2,1)}, u32[]{:S(2)}, u32[]{:S(2)}) collective-permute-start(bf16[1024,1152]{1,0:T(8,128)(2,1)} %get-tuple-element.26.refs_0_.own), channel_id=1, source_target_pairs={{0,1},{1,0},{2,3},{3,2},{4,5},{5,4},{6,7},{7,6},{8,9},{9,8},{10,11... | collective-permute-start | bytes 7077896 | tf_op jit(solution)/shard_map/near/ppermute | solution.py:78
  10.1 33.3 %collective-permute-start.3 = (bf16[512,1152]{1,0:T(8,128)(2,1)}, bf16[512,1152]{1,0:T(8,128)(2,1)}, u32[]{:S(2)}, u32[]{:S(2)}) collective-permute-start(bf16[512,1152]{1,0:T(8,128)(2,1)} %get-tuple-element.29), channel_id=1, source_target_pairs={{0,8},{1,25},{2,10},{3,27},{4,28},{5,13},{6,30},{7,15},{8,0},{9,17... | collective-permute-start | bytes 3538952 | tf_op jit(solution)/shard_map/a_01/ppermute | solution.py:78
  11.4 32.0 %collective-permute-start.4 = (bf16[512,1152]{1,0:T(8,128)(2,1)S(1)}, bf16[512,1152]{1,0:T(8,128)(2,1)}, u32[]{:S(2)}, u32[]{:S(2)}) collective-permute-start(bf16[512,1152]{1,0:T(8,128)(2,1)S(1)} %get-tuple-element.30), channel_id=1, source_target_pairs={{0,24},{1,9},{2,26},{3,11},{4,12},{5,29},{6,14},{7,31},{8,16},{9,1... | collective-permute-start | bytes 3538952 | tf_op jit(solution)/shard_map/b_01/ppermute | solution.py:78
  14.8 1.7 %copy-start.1 = (bf16[1024,1152]{1,0:T(8,128)(2,1)S(1)}, bf16[1024,1152]{1,0:T(8,128)(2,1)}, u32[]{:S(2)}) copy-start(bf16[1024,1152]{1,0:T(8,128)(2,1)} %get-tuple-element.25.own.refs_0_) | copy-start | bytes 7077892
  16.5 9.9 %copy-start = (bf16[1024,1152]{1,0:T(8,128)(2,1)S(1)}, bf16[1024,1152]{1,0:T(8,128)(2,1)}, u32[]{:S(2)}) copy-start(bf16[1024,1152]{1,0:T(8,128)(2,1)} %get-tuple-element.26.refs_0_.own) | copy-start | bytes 7077892
  43.3 26.6 %collective-permute-start.1 = (bf16[512,1152]{1,0:T(8,128)(2,1)}, bf16[512,1152]{1,0:T(8,128)(2,1)}, u32[]{:S(2)}, u32[]{:S(2)}) collective-permute-start(bf16[512,1152]{1,0:T(8,128)(2,1)} %get-tuple-element.27), channel_id=1, source_target_pairs={{0,8},{1,25},{2,10},{3,27},{4,28},{5,13},{6,30},{7,15},{8,0},{9,17... | collective-permute-start | bytes 3538952 | tf_op jit(solution)/shard_map/a_11/ppermute | solution.py:78
  43.8 29.4 %collective-permute-start.2 = (bf16[512,1152]{1,0:T(8,128)(2,1)}, bf16[512,1152]{1,0:T(8,128)(2,1)}, u32[]{:S(2)}, u32[]{:S(2)}) collective-permute-start(bf16[512,1152]{1,0:T(8,128)(2,1)} %get-tuple-element.28), channel_id=1, source_target_pairs={{0,24},{1,9},{2,26},{3,11},{4,12},{5,29},{6,14},{7,31},{8,16},{9,1... | collective-permute-start | bytes 3538952 | tf_op jit(solution)/shard_map/b_11/ppermute | solution.py:78
  47.1 27.0 %collective-permute-start.6 = (bf16[512,1152]{1,0:T(8,128)(2,1)}, bf16[512,1152]{1,0:T(8,128)(2,1)S(1)}, u32[]{:S(2)}, u32[]{:S(2)}) collective-permute-start(bf16[512,1152]{1,0:T(8,128)(2,1)} %broadcast_select_fusion.1), channel_id=1, source_target_pairs={{0,6},{1,3},{2,0},{3,5},{4,2},{5,7},{6,4},{7,1},{8,14},{9,11},{10,... | collective-permute-start | bytes 3538952 | tf_op jit(solution)/shard_map/a_x0/ppermute | solution.py:78
  48.8 39.5 %collective-permute-start.5 = (bf16[512,1152]{1,0:T(8,128)(2,1)S(1)}, bf16[512,1152]{1,0:T(8,128)(2,1)S(1)}, u32[]{:S(2)}, u32[]{:S(2)}) collective-permute-start(bf16[512,1152]{1,0:T(8,128)(2,1)S(1)} %broadcast_select_fusion.3), channel_id=1, source_target_pairs={{0,2},{1,7},{2,4},{3,1},{4,6},{5,3},{6,0},{7,5},{8,10},{9,15},{10,... | collective-permute-start | bytes 3538952 | tf_op jit(solution)/shard_map/b_x0/ppermute | solution.py:78
  73.2 30.2 %collective-permute-start.8 = (bf16[512,1152]{1,0:T(8,128)(2,1)}, bf16[512,1152]{1,0:T(8,128)(2,1)S(1)}, u32[]{:S(2)}, u32[]{:S(2)}) collective-permute-start(bf16[512,1152]{1,0:T(8,128)(2,1)} %collective-permute-done.3), channel_id=1, source_target_pairs={{0,120},{1,41},{2,122},{3,43},{4,12},{5,29},{6,14},{7,31},{8,112},... | collective-permute-start | bytes 3538952 | tf_op jit(solution)/shard_map/a_02/ppermute | solution.py:78
  74.1 29.4 %collective-permute-start.9 = (bf16[512,1152]{1,0:T(8,128)(2,1)}, bf16[512,1152]{1,0:T(8,128)(2,1)S(1)}, u32[]{:S(2)}, u32[]{:S(2)}) collective-permute-start(bf16[512,1152]{1,0:T(8,128)(2,1)} %collective-permute-done.4), channel_id=1, source_target_pairs={{0,40},{1,121},{2,42},{3,123},{4,28},{5,13},{6,30},{7,15},{8,32},{... | collective-permute-start | bytes 3538952 | tf_op jit(solution)/shard_map/b_02/ppermute | solution.py:78
  74.1 15.7 %collective-permute-start.7 = (bf16[512,1152]{1,0:T(8,128)(2,1)S(1)}, bf16[512,1152]{1,0:T(8,128)(2,1)S(1)}, u32[]{:S(2)}, u32[]{:S(2)}) collective-permute-start(bf16[512,1152]{1,0:T(8,128)(2,1)S(1)} %collective-permute-done.6.refs_0_), channel_id=1, source_target_pairs={{0,1},{1,0},{2,3},{3,2},{4,5},{5,4},{6,7},{7,6},{8,9},{9,8},{10,11... | collective-permute-start | bytes 3538952 | tf_op jit(solution)/shard_map/far_0/ppermute | solution.py:78
  79.8 23.6 %collective-permute-start.13 = (bf16[512,1152]{1,0:T(8,128)(2,1)S(1)}, bf16[512,1152]{1,0:T(8,128)(2,1)S(1)}, u32[]{:S(2)}, u32[]{:S(2)}) collective-permute-start(bf16[512,1152]{1,0:T(8,128)(2,1)S(1)} %broadcast_select_fusion), channel_id=1, source_target_pairs={{0,6},{1,3},{2,0},{3,5},{4,2},{5,7},{6,4},{7,1},{8,14},{9,11},{10,... | collective-permute-start | bytes 3538952 | tf_op jit(solution)/shard_map/a_x1/ppermute | solution.py:78
  88.3 30.3 %collective-permute-start.12 = (bf16[512,1152]{1,0:T(8,128)(2,1)S(1)}, bf16[512,1152]{1,0:T(8,128)(2,1)S(1)}, u32[]{:S(2)}, u32[]{:S(2)}) collective-permute-start(bf16[512,1152]{1,0:T(8,128)(2,1)S(1)} %broadcast_select_fusion.2), channel_id=1, source_target_pairs={{0,2},{1,7},{2,4},{3,1},{4,6},{5,3},{6,0},{7,5},{8,10},{9,15},{10,... | collective-permute-start | bytes 3538952 | tf_op jit(solution)/shard_map/b_x1/ppermute | solution.py:78
  103.4 15.2 %collective-permute-start.14 = (bf16[512,1152]{1,0:T(8,128)(2,1)S(1)}, bf16[512,1152]{1,0:T(8,128)(2,1)S(1)}, u32[]{:S(2)}, u32[]{:S(2)}) collective-permute-start(bf16[512,1152]{1,0:T(8,128)(2,1)S(1)} %collective-permute-done.13.refs_1_), channel_id=1, source_target_pairs={{0,1},{1,0},{2,3},{3,2},{4,5},{5,4},{6,7},{7,6},{8,9},{9,8},{10,11... | collective-permute-start | bytes 3538952 | tf_op jit(solution)/shard_map/far_1/ppermute | solution.py:78
  105.1 27.4 %collective-permute-start.10 = (bf16[512,1152]{1,0:T(8,128)(2,1)}, bf16[512,1152]{1,0:T(8,128)(2,1)S(1)}, u32[]{:S(2)}, u32[]{:S(2)}) collective-permute-start(bf16[512,1152]{1,0:T(8,128)(2,1)} %collective-permute-done.2), channel_id=1, source_target_pairs={{0,40},{1,121},{2,42},{3,123},{4,28},{5,13},{6,30},{7,15},{8,32},{... | collective-permute-start | bytes 3538952 | tf_op jit(solution)/shard_map/b_12/ppermute | solution.py:78
  105.1 31.5 %collective-permute-start.11 = (bf16[512,1152]{1,0:T(8,128)(2,1)}, bf16[512,1152]{1,0:T(8,128)(2,1)S(1)}, u32[]{:S(2)}, u32[]{:S(2)}) collective-permute-start(bf16[512,1152]{1,0:T(8,128)(2,1)} %collective-permute-done.1), channel_id=1, source_target_pairs={{0,120},{1,41},{2,122},{3,43},{4,12},{5,29},{6,14},{7,31},{8,112},... | collective-permute-start | bytes 3538952 | tf_op jit(solution)/shard_map/a_12/ppermute | solution.py:78
  118.6 18.1 %copy-start.4 = (f32[1024,1]{1,0:T(8,128)S(1)}, f32[1024,1]{1,0:T(8,128)}, u32[]{:S(2)}) copy-start(f32[1024,1]{1,0:T(8,128)} %copy-done.3) | copy-start | bytes 12292
  118.6 18.1 %copy-start.6 = (f32[1024,1]{1,0:T(8,128)S(1)}, f32[1024,1]{1,0:T(8,128)}, u32[]{:S(2)}) copy-start(f32[1024,1]{1,0:T(8,128)} %copy-done.5) | copy-start | bytes 12292
